TPU v7x, 32 devices: a whole 2x2x4 slice. The times are simulated.
32 devices in a mesh: dp: 8 (over y, x, core), expert: 4 (over z).
Axes of the slice: x: 2, y: 2, z: 4, core: 2. Of those that a mesh axis runs over, the one named last changes fastest.
Arguments:
- tokens: bfloat16 [512, 2048], P(('dp', 'expert')), may hold values from -6 to 6
- out_grad: bfloat16 [512, 2048], P(('dp', 'expert')), may hold values from -6 to 6
- gate_weights: bfloat16 [512, 2], P(('dp', 'expert')), may hold values from 0.049804688 to 1
- expert_ids: int32 [512, 2], P(('dp', 'expert')), may hold values from 0 to 3, all different within a row; in each aligned block of 16 rows (0 to 15, 16 to 31, ...) at most 10 rows name the same one
- swapped: int32 [4], replicated, may hold values from 0 to 1, as said below
- up_weight: bfloat16 [4, 2048, 384], P('expert'), may hold values from -0.125 to 0.125
- down_weight: bfloat16 [4, 384, 2048], P('expert'), may hold values from -0.3125 to 0.3125
Outputs:
- layer_out: bfloat16 [512, 2048], P(('dp', 'expert'))
- token_grad: bfloat16 [512, 2048], P(('dp', 'expert'))
- up_grad: float32 [4, 2048, 384], P('expert', 'dp')
- down_grad: float32 [4, 384, 2048], P('expert', 'dp')
Inputs may be any that keep to these rules, and one draw needn't show every extreme that they name: swapped[s] equals swapped[(s + 2) mod 4]; swapped[0] is 1. `expert_ids`: A token's 2 experts differ; at most 10 of the tokens of one device name one expert, and that many in some device.
All inputs are finite; a program needn't handle non-finite values.
Results may differ from a plain program's by a relative error of at most 0.023.
Values may be sent and summed in bfloat16 or wider, within the bound.
A program may use at most 64 MiB of HBM per device.

v0:
```python
import functools

import jax
import jax.numpy as jnp
from jax import lax
from jax.experimental import pallas as pl
from jax.experimental.pallas import tpu as pltpu
from jax.sharding import PartitionSpec as P

BF = jnp.bfloat16
F32 = jnp.float32


def by_collectives(tokens, out_grad, gate_weights, expert_ids, swapped, up_weight, down_weight):
    owners = lax.axis_size("expert")
    mine = lax.axis_index("expert")
    width = tokens.shape[1]
    lanes = jnp.arange(128, dtype=jnp.int32)
    hit = expert_ids[:, :, None] == lanes[None, None, :]
    gates = jnp.sum(jnp.where(hit, gate_weights.astype(F32)[:, :, None], 0.0), axis=1).astype(BF)
    packed = jnp.concatenate([tokens, out_grad, gates], axis=1)
    full = lax.all_gather(packed, "expert", axis=0, tiled=True)
    x, og, gates = full[:, :width], full[:, width : 2 * width], full[:, 2 * width :]
    gates = gates.astype(F32)
    flag = lax.dynamic_slice_in_dim(swapped, mine, 1, 0)[0] == 1
    held = jnp.where(flag, (mine + owners // 2) % owners, mine)

    def column(e):
        return jnp.sum(jnp.where(lanes[None, :] == e, gates, 0.0), axis=1, keepdims=True)

    gate = column(mine)
    up, down = up_weight[0], down_weight[0]
    dy = (gate * og.astype(F32)).astype(BF)
    hidden = jnp.dot(x, up, preferred_element_type=F32)
    d_active = lax.dot_general(dy, down, (((1,), (1,)), ((), ())), preferred_element_type=F32)
    sigma = jax.nn.sigmoid(hidden)
    active = jnp.where(gate > 0, hidden * sigma, 0.0).astype(BF)
    d_hidden = (d_active * sigma * (1.0 + hidden * (1.0 - sigma))).astype(BF)
    other = lax.ppermute(
        jnp.concatenate([active, d_hidden], axis=1),
        "expert",
        [(i, (i + owners // 2) % owners) for i in range(owners)],
    )
    y = jnp.dot(active, down, preferred_element_type=F32).astype(BF).astype(F32)
    dx = lax.dot_general(d_hidden, up, (((1,), (1,)), ((), ())), preferred_element_type=F32)
    back = jnp.concatenate([(gate * y).astype(BF), dx.astype(BF)], axis=1)
    back = lax.psum_scatter(back, "expert", scatter_dimension=0, tiled=True)
    fw = active.shape[1]
    act_h = jnp.where(flag, other[:, :fw], active)
    dh_h = jnp.where(flag, other[:, fw:], d_hidden)
    dy_h = (column(held) * og.astype(F32)).astype(BF)
    over = (((0,), (0,)), ((), ()))
    part_up = lax.dot_general(x, dh_h, over, preferred_element_type=F32).astype(BF)
    part_down = lax.dot_general(act_h, dy_h, over, preferred_element_type=F32).astype(BF)
    sum_up = lax.psum_scatter(part_up, "dp", scatter_dimension=0, tiled=True).astype(F32)
    sum_down = lax.psum_scatter(part_down, "dp", scatter_dimension=0, tiled=True).astype(F32)
    return back[:, :width], back[:, width:], sum_up[None], sum_down[None]


NT = (((1,), (1,)), ((), ()))
TN = (((0,), (0,)), ((), ()))


def dot(a, b, dims=(((1,), (0,)), ((), ()))):
    return lax.dot_general(a, b, dims, preferred_element_type=F32)


def kernel(
    groups,
    owners,
    swapped_ref,
    tok_ref,
    og_ref,
    gate_ref,
    ids_ref,
    up_ref,
    down_ref,
    out_ref,
    tgrad_ref,
    ugrad_ref,
    dgrad_ref,
    xs,
    ogs,
    gs,
    up_buf,
    down_buf,
    dy_out,
    x_in,
    dy_in,
    own,
    other,
    picked,
    y_out,
    y_in,
    dx_out,
    dx_in,
    down_out,
    down_in,
    load,
    z_send,
    z_recv,
    dp_send,
    dp_recv,
    swap_send,
    swap_recv,
    pair_send,
    out_buf,
    tgrad_buf,
    ugrad_buf,
    dgrad_buf,
    store,
    line_send,
):
    tok, width = tok_ref.shape
    fw = up_ref.shape[2]
    part = width // groups
    depth = fw // groups
    count = owners * tok
    me = lax.axis_index("expert")
    group = lax.axis_index("dp")
    half = owners // 2
    twin = group + 1 - 2 * lax.rem(group, 2)

    def z_peer(k):
        return lax.rem(me + k, owners)

    def dp_peer(k):
        return lax.rem(group + k, groups)

    def cols(p):
        return pl.ds(pl.multiple_of(p * part, 128), part)

    def send(src, dst, s, r, **where):
        return pltpu.make_async_remote_copy(
            src_ref=src,
            dst_ref=dst,
            send_sem=s,
            recv_sem=r,
            device_id=where,
            device_id_type=pl.DeviceIdType.MESH,
        )

    barrier = pltpu.get_barrier_semaphore()
    for k in range(1, owners):
        pl.semaphore_signal(
            barrier, inc=1, device_id={"expert": z_peer(k)}, device_id_type=pl.DeviceIdType.MESH
        )
    for k in range(1, groups):
        pl.semaphore_signal(
            barrier, inc=1, device_id={"dp": dp_peer(k)}, device_id_type=pl.DeviceIdType.MESH
        )
    loads = [
        pltpu.make_async_copy(tok_ref, xs.at[me], load.at[0]),
        pltpu.make_async_copy(og_ref, ogs.at[me], load.at[1]),
        pltpu.make_async_copy(up_ref.at[0], up_buf, load.at[2]),
        pltpu.make_async_copy(down_ref.at[0], down_buf, load.at[3]),
    ]
    for copy in loads:
        copy.start()
    lines = lax.broadcasted_iota(jnp.int32, (128, tok), 0)
    dense = jnp.zeros((128, tok), F32)
    for k in range(ids_ref.shape[0]):
        hit = ids_ref[k : k + 1, :] == lines
        dense += jnp.where(hit, gate_ref[k : k + 1, :].astype(F32), 0.0)
    eye = (
        lax.broadcasted_iota(jnp.int32, (128, 128), 0)
        == lax.broadcasted_iota(jnp.int32, (128, 128), 1)
    ).astype(BF)
    gs[me] = dot(dense.astype(BF), eye, TN).astype(BF)
    flag = swapped_ref[me]
    held = jnp.where(flag == 1, lax.rem(me + half, owners), me)
    pl.semaphore_wait(barrier, owners + groups - 2)

    started = []

    def start(copy):
        copy.start()
        started.append(copy)

    order = sorted(range(1, owners), key=lambda k: -min(k, owners - k))
    blocks = ((tok_ref, xs), (gs.at[me], gs), (og_ref, ogs))
    handed = []

    def hand_on(n, src, b, cond, way):
        copy = send(
            src,
            blocks[n][1].at[b],
            line_send.at[way, n, b],
            z_recv.at[n, b],
            expert=lax.rem(me + owners + 1 - 2 * way, owners),
        )

        @pl.when(cond)
        def _():
            copy.start()

        handed.append((cond, copy))

    for n, (src, dst) in enumerate(blocks):
        hand_on(n, src, me, me < owners - 1, 0)
        hand_on(n, src, me, me > 0, 1)

    def arrive(n, d):
        dst = blocks[n][1]
        for way, there, on in (
            (0, me >= d, me < owners - 1),
            (1, me < owners - d, me > 0),
        ):
            b = lax.rem(me + owners - d if way == 0 else me + d, owners)

            @pl.when(there)
            def _():
                send(
                    dst.at[b], dst.at[b], line_send.at[way, n, b], z_recv.at[n, b], expert=b
                ).wait_recv()

            if d < owners - 1:
                hand_on(n, dst.at[b], b, jnp.logical_and(there, on), way)

    for d in range(1, owners - 1):
        for n in range(3):
            arrive(n, d)
    last = owners - 1
    loads[0].wait()
    arrive(0, last)
    for k in range(1, groups):
        p = dp_peer(k)
        start(
            send(xs.at[:, :, cols(p)], x_in.at[group], dp_send.at[0, k], dp_recv.at[0, group], dp=p)
        )
    x_in[group] = xs[:, :, cols(group)]
    loads[2].wait()
    up = up_buf[...]
    hidden = dot(xs[...].reshape(count, width), up)
    sigma = 1.0 / (1.0 + jnp.exp(-hidden))
    arrive(1, last)
    gates = gs[...].reshape(count, 128).astype(F32)
    lane = lax.broadcasted_iota(jnp.int32, (count, 128), 1)

    def column(e):
        return jnp.sum(jnp.where(lane == e, gates, 0.0), axis=1, keepdims=True)

    gate, gate_held = column(me), column(held)
    active = jnp.where(gate > 0, hidden * sigma, 0.0).astype(BF)
    own[:, :fw] = active
    loads[1].wait()
    loads[3].wait()
    down = down_buf[...]
    arrive(2, last)
    og = ogs[...].reshape(count, width).astype(F32)
    d_active = dot((gate * og).astype(BF), down, NT)
    d_hidden = (d_active * sigma * (1.0 + hidden * (1.0 - sigma))).astype(BF)
    own[:, fw:] = d_hidden
    swap = send(own, other, swap_send, swap_recv, expert=lax.rem(me + half, owners))
    start(swap)
    dy_out[...] = (gate_held * og).astype(BF).reshape(owners, tok, width)
    for k in range(1, groups):
        p = dp_peer(k)
        start(
            send(
                dy_out.at[:, :, cols(p)], dy_in.at[group], dp_send.at[1, k], dp_recv.at[1, group], dp=p
            )
        )
    dy_in[group] = dy_out[:, :, cols(group)]
    y = dot(active, down).astype(BF).astype(F32)
    y_out[...] = (gate * y).astype(BF).reshape(owners, tok, width)
    dx_out[...] = dot(d_hidden, up, NT).astype(BF).reshape(owners, tok, width)

    swap.wait_recv()
    picked[group] = jnp.where(flag == 1, other[...], own[...])
    mine = picked.at[group]
    for k in range(2, groups, 2):
        start(send(mine, mine, dp_send.at[2, k], dp_recv.at[2, group], dp=dp_peer(k)))
    start(send(mine, mine, dp_send.at[2, 0], dp_recv.at[2, group], dp=twin))
    for k in order:
        p = z_peer(k)
        start(send(y_out.at[p], y_in.at[me], z_send.at[3, k], z_recv.at[3, me], expert=p))
    for k in order:
        p = z_peer(k)
        start(send(dx_out.at[p], dx_in.at[me], z_send.at[4, k], z_recv.at[4, me], expert=p))
    for k in range(2, groups, 2):
        p = dp_peer(k)
        block = picked.at[p]
        send(block, block, dp_send.at[2, k], dp_recv.at[2, p], dp=p).wait_recv()
        start(send(block, block, pair_send.at[k], dp_recv.at[2, p], dp=twin))
    for n, dst in ((0, x_in), (1, dy_in)):
        for k in range(1, groups):
            p = dp_peer(k)
            send(dst.at[p], dst.at[p], dp_send.at[n, k], dp_recv.at[n, p], dp=p).wait_recv()
    for k in range(0, groups, 2):
        p = lax.rem(twin + k, groups)
        block = picked.at[p]
        send(block, block, dp_send.at[2, k], dp_recv.at[2, p], dp=twin).wait_recv()

    total = groups * count
    act_all = picked[:, :, :fw].reshape(total, fw)
    dy_all = dy_in[...].reshape(total, part)
    down_out[...] = dot(act_all, dy_all, TN).astype(BF).reshape(groups, depth, part)
    for k in range(1, groups):
        p = dp_peer(k)
        start(send(down_out.at[p], down_in.at[group], dp_send.at[3, k], dp_recv.at[3, group], dp=p))
    down_in[group] = down_out[group]
    dh_all = picked[:, :, fw:].reshape(total, fw)
    ugrad_buf[0] = dot(x_in[...].reshape(total, part), dh_all, TN)
    stores = [
        pltpu.make_async_copy(src, dst, store.at[i])
        for i, (src, dst) in enumerate(
            ((out_buf, out_ref), (tgrad_buf, tgrad_ref), (ugrad_buf, ugrad_ref), (dgrad_buf, dgrad_ref))
        )
    ]
    stores[2].start()

    for n, out, src, dst in ((3, out_buf, y_out, y_in), (4, tgrad_buf, dx_out, dx_in)):
        acc = src[me].astype(F32)
        for k in range(1, owners):
            p = z_peer(k)
            send(src.at[p], dst.at[p], z_send.at[n, k], z_recv.at[n, p], expert=p).wait_recv()
            acc += dst[p].astype(F32)
        out[...] = acc.astype(BF)
        stores[n - 3].start()
    for k in range(1, groups):
        p = dp_peer(k)
        send(down_out.at[p], down_in.at[p], dp_send.at[3, k], dp_recv.at[3, p], dp=p).wait_recv()
    for j in range(groups):
        dgrad_buf[0, :, j * part : (j + 1) * part] = down_in[j].astype(F32)
    stores[3].start()
    for copy in started:
        copy.wait_send()
    for cond, copy in handed:

        @pl.when(cond)
        def _(copy=copy):
            copy.wait_send()

    for copy in stores:
        copy.wait()


def place(*refs):
    count = (len(refs) - 2) // 3
    loaded, stored = refs[-2:]
    ins, outs, bufs = refs[:count], refs[count : 2 * count], refs[2 * count : 3 * count]
    loads = [pltpu.make_async_copy(ins[i], bufs[i], loaded.at[i]) for i in range(count)]
    stores = [pltpu.make_async_copy(bufs[i], outs[i], stored.at[i]) for i in range(count)]
    for copy in loads:
        copy.start()
    for load, store in zip(loads, stores):
        load.wait()
        store.start()
    for copy in stores:
        copy.wait()


def by_kernel(groups, owners, tokens, out_grad, gate_weights, expert_ids, swapped, up, down):
    tok, width = tokens.shape
    fw = up.shape[2]
    part, depth, count = width // groups, fw // groups, owners * tok
    vmem = pl.BlockSpec(memory_space=pltpu.VMEM)
    hbm = pl.BlockSpec(memory_space=pltpu.HBM)
    dma = pltpu.SemaphoreType.DMA
    shapes = (
        jax.ShapeDtypeStruct((tok, width), BF),
        jax.ShapeDtypeStruct((tok, width), BF),
        jax.ShapeDtypeStruct((1, part, fw), F32),
        jax.ShapeDtypeStruct((1, depth, width), F32),
    )
    wide = pltpu.VMEM((owners, tok, width), BF)
    slim = pltpu.VMEM((groups, owners, tok, part), BF)
    hid = pltpu.VMEM((count, 2 * fw), BF)
    results = pl.pallas_call(
        functools.partial(kernel, groups, owners),
        out_shape=shapes,
        in_specs=[pl.BlockSpec(memory_space=pltpu.SMEM), hbm, hbm, vmem, vmem, hbm, hbm],
        out_specs=(hbm,) * 4,
        scratch_shapes=[
            wide,
            wide,
            pltpu.VMEM((owners, tok, 128), BF),
            pltpu.VMEM(up.shape[1:], BF),
            pltpu.VMEM(down.shape[1:], BF),
            wide,
            slim,
            slim,
            hid,
            hid,
            pltpu.VMEM((groups, count, 2 * fw), BF),
            wide,
            wide,
            wide,
            wide,
            pltpu.VMEM((groups, depth, part), BF),
            pltpu.VMEM((groups, depth, part), BF),
            dma((4,)),
            dma((5, owners)),
            dma((5, owners)),
            dma((4, groups)),
            dma((4, groups)),
            dma(()),
            dma(()),
            dma((groups,)),
            *[pltpu.VMEM(a.shape, a.dtype) for a in shapes],
            dma((4,)),
            dma((2, 3, owners)),
        ],
        compiler_params=pltpu.CompilerParams(
            collective_id=0, has_side_effects=True, vmem_limit_bytes=62 << 20
        ),
    )(swapped, tokens, out_grad, gate_weights.T, expert_ids.T, up, down)
    return pl.pallas_call(
        place,
        out_shape=shapes,
        in_specs=[pl.BlockSpec(memory_space=pl.ANY)] * 4,
        out_specs=(hbm,) * 4,
        scratch_shapes=[pltpu.VMEM(a.shape, a.dtype) for a in shapes] + [dma((4,)), dma((4,))],
        compiler_params=pltpu.CompilerParams(vmem_limit_bytes=62 << 20),
    )(*results)


def solution(mesh):
    groups, owners = mesh.shape["dp"], mesh.shape["expert"]

    def on_device(tokens, out_grad, gate_weights, expert_ids, swapped, up_weight, down_weight):
        args = (tokens, out_grad, gate_weights, expert_ids, swapped, up_weight, down_weight)
        width, fw = tokens.shape[1], up_weight.shape[2]
        if width % (128 * groups) == 0 and fw % (16 * groups) == 0:
            return by_kernel(groups, owners, *args)
        return by_collectives(*args)

    rows = P(("dp", "expert"), None)
    in_specs = (rows, rows, rows, rows, P(), P("expert", None, None), P("expert", None, None))
    out_specs = (rows, rows, P("expert", "dp", None), P("expert", "dp", None))
    return jax.shard_map(
        on_device, mesh=mesh, in_specs=in_specs, out_specs=out_specs, check_vma=False
    )
```

profile of v0, /device:TPU:0, one launch (start us, length us, event | category | flops | bytes accessed | tf_op | source)
XLA Modules:
  0.0 39.3 jit_solution(17267978226044410312)
XLA Ops:
  0.6 36.7 %shard_map.102 = (bf16[16,2048]{1,0:T(8,128)(2,1)}, bf16[16,2048]{1,0:T(8,128)(2,1)}, f32[1,256,384]{2,1,0:T(8,128)}, f32[1,48,2048]{2,1,0:T(8,128)}) custom-call(s32[4]{0:T(128)} %swapped_ref.1, bf16[16,2048]{1,0:T(8,128)(2,1)} %tok_ref.1, bf16[16,2048]{1,0:T(8,128)(2,1)} %og_ref.1, bf16[2,16]{1,0:T(2,128)(2,1)} %bitcast.3, s32[2,16]{1,0:T(2,128)} %bitcast.2, ...), custom_call_target="tpu_custom_call" | custom-call | tf_op jit(solution)/shard_map/pallas_call | solution.py:370
  37.3 2.0 %shard_map.103 = (bf16[16,2048]{1,0:T(8,128)(2,1)}, bf16[16,2048]{1,0:T(8,128)(2,1)}, f32[1,256,384]{2,1,0:T(8,128)}, f32[1,48,2048]{2,1,0:T(8,128)}) custom-call(bf16[16,2048]{1,0:T(8,128)(2,1)} %get-tuple-element.8.refs_0_, bf16[16,2048]{1,0:T(8,128)(2,1)} %get-tuple-element.9.refs_1_, f32[1,256,384]{2,1,0:T(8,128)} %get-tuple-element.10.refs_2_, ...), custom_call_target="tpu_custom_call" | custom-call | tf_op jit(solution)/shard_map/pallas_call | solution.py:409
where the time goes:
time: 39.5 us; the launch traced here: 39.3 us
  Pallas kernels  38.7 us (98%)
  between operations  0.64 us (2%)
    pallas_call x1, Pallas kernels, by_kernel(): pl.pallas_call(functools.partial(kernel, groups, owners), out_shape=shape...  36.7 us
    pallas_call x1, Pallas kernels, by_kernel(): pl.pallas_call(place, out_shape=shapes, in_specs=[pl.BlockSpec(memory_spa...  2.02 us

commit v1 on v0

v1 whole, which is shorter than its diff:
```python
import functools

import jax
import jax.numpy as jnp
from jax import lax
from jax.experimental import pallas as pl
from jax.experimental.pallas import tpu as pltpu
from jax.sharding import PartitionSpec as P

BF = jnp.bfloat16
F32 = jnp.float32


def by_collectives(tokens, out_grad, gate_weights, expert_ids, swapped, up_weight, down_weight):
    owners = lax.axis_size("expert")
    mine = lax.axis_index("expert")
    width = tokens.shape[1]
    lanes = jnp.arange(128, dtype=jnp.int32)
    hit = expert_ids[:, :, None] == lanes[None, None, :]
    gates = jnp.sum(jnp.where(hit, gate_weights.astype(F32)[:, :, None], 0.0), axis=1).astype(BF)
    packed = jnp.concatenate([tokens, out_grad, gates], axis=1)
    full = lax.all_gather(packed, "expert", axis=0, tiled=True)
    x, og, gates = full[:, :width], full[:, width : 2 * width], full[:, 2 * width :]
    gates = gates.astype(F32)
    flag = lax.dynamic_slice_in_dim(swapped, mine, 1, 0)[0] == 1
    held = jnp.where(flag, (mine + owners // 2) % owners, mine)

    def column(e):
        return jnp.sum(jnp.where(lanes[None, :] == e, gates, 0.0), axis=1, keepdims=True)

    gate = column(mine)
    up, down = up_weight[0], down_weight[0]
    dy = (gate * og.astype(F32)).astype(BF)
    hidden = jnp.dot(x, up, preferred_element_type=F32)
    d_active = lax.dot_general(dy, down, (((1,), (1,)), ((), ())), preferred_element_type=F32)
    sigma = jax.nn.sigmoid(hidden)
    active = jnp.where(gate > 0, hidden * sigma, 0.0).astype(BF)
    d_hidden = (d_active * sigma * (1.0 + hidden * (1.0 - sigma))).astype(BF)
    other = lax.ppermute(
        jnp.concatenate([active, d_hidden], axis=1),
        "expert",
        [(i, (i + owners // 2) % owners) for i in range(owners)],
    )
    y = jnp.dot(active, down, preferred_element_type=F32).astype(BF).astype(F32)
    dx = lax.dot_general(d_hidden, up, (((1,), (1,)), ((), ())), preferred_element_type=F32)
    back = jnp.concatenate([(gate * y).astype(BF), dx.astype(BF)], axis=1)
    back = lax.psum_scatter(back, "expert", scatter_dimension=0, tiled=True)
    fw = active.shape[1]
    act_h = jnp.where(flag, other[:, :fw], active)
    dh_h = jnp.where(flag, other[:, fw:], d_hidden)
    dy_h = (column(held) * og.astype(F32)).astype(BF)
    over = (((0,), (0,)), ((), ()))
    part_up = lax.dot_general(x, dh_h, over, preferred_element_type=F32).astype(BF)
    part_down = lax.dot_general(act_h, dy_h, over, preferred_element_type=F32).astype(BF)
    sum_up = lax.psum_scatter(part_up, "dp", scatter_dimension=0, tiled=True).astype(F32)
    sum_down = lax.psum_scatter(part_down, "dp", scatter_dimension=0, tiled=True).astype(F32)
    return back[:, :width], back[:, width:], sum_up[None], sum_down[None]


NT = (((1,), (1,)), ((), ()))
TN = (((0,), (0,)), ((), ()))


def dot(a, b, dims=(((1,), (0,)), ((), ()))):
    return lax.dot_general(a, b, dims, preferred_element_type=F32)


X_IN, OG_IN, X_OWN, OG_OWN, X_REST, OG_REST = 0, 3, 6, 7, 8, 9
SWAP_ACT, SWAP_DH, ACT_IN, ACT_TWIN, DH_IN, DH_TWIN, DOWN, Y, DX = 10, 11, 12, 15, 16, 19, 20, 21, 22
ARRIVALS = 23
(
    S_X,
    S_OG,
    S_X_OWN,
    S_OG_OWN,
    S_X_REST,
    S_OG_REST,
    S_SWAP_ACT,
    S_SWAP_DH,
    S_ACT,
    S_DH,
    S_DOWN,
    S_Y,
    S_DX,
) = range(13)
DEPARTURES = 13


def kernel(
    swapped_ref,
    tok_ref,
    og_ref,
    gate_ref,
    ids_ref,
    up_ref,
    down_ref,
    out_ref,
    tgrad_ref,
    ugrad_ref,
    dgrad_ref,
    xs,
    ogs,
    up_buf,
    down_buf,
    x_in,
    og_in,
    own_act,
    own_dh,
    other_act,
    other_dh,
    act_all,
    dh_all,
    y_out,
    y_in,
    dx_out,
    dx_in,
    down_out,
    down_in,
    load,
    left,
    came,
):
    owners, groups = 4, 8
    tok, width = tok_ref.shape
    fw = up_ref.shape[2]
    part, depth, half, eighth = width // groups, fw // groups, width // 2, width // 8
    count = owners * tok
    me = lax.axis_index("expert")
    group = lax.axis_index("dp")
    chip, core = group // 2, lax.rem(group, 2)
    middle = jnp.logical_or(me == 1, me == 2)
    twin = 2 * chip + 1 - core

    def peer(f):
        return 2 * lax.rem(chip + f % 4, 4) + lax.rem(core + f // 4, 2)

    def back(f):
        return f // 4 * 4 + (4 - f % 4) % 4

    def cols(p):
        return pl.ds(pl.multiple_of(p * part, 128), part)

    def z_peer(k):
        return lax.rem(me + k, owners)

    def send(src, dst, s, r, **where):
        return pltpu.make_async_remote_copy(
            src_ref=src,
            dst_ref=dst,
            send_sem=left.at[s],
            recv_sem=came.at[r],
            device_id=where,
            device_id_type=pl.DeviceIdType.MESH,
        )

    def arrived(dst, r):
        send(dst, dst, 0, r, dp=twin).wait_recv()

    def departed(src, s):
        send(src, src, s, 0, dp=twin).wait_send()

    barrier = pltpu.get_barrier_semaphore()
    for k in range(1, owners):
        pl.semaphore_signal(
            barrier, inc=1, device_id={"expert": z_peer(k)}, device_id_type=pl.DeviceIdType.MESH
        )
    for f in range(1, groups):
        pl.semaphore_signal(
            barrier, inc=1, device_id={"dp": peer(f)}, device_id_type=pl.DeviceIdType.MESH
        )
    loads = [
        pltpu.make_async_copy(tok_ref, xs.at[0, :, pl.ds(0, width)], load.at[0]),
        pltpu.make_async_copy(og_ref, ogs.at[0], load.at[1]),
        pltpu.make_async_copy(up_ref.at[0], up_buf, load.at[2]),
        pltpu.make_async_copy(down_ref.at[0], down_buf, load.at[3]),
    ]
    for copy in loads:
        copy.start()
    lines = lax.broadcasted_iota(jnp.int32, (128, tok), 0)
    dense = jnp.zeros((128, tok), F32)
    for k in range(ids_ref.shape[0]):
        hit = ids_ref[k : k + 1, :] == lines
        dense += jnp.where(hit, gate_ref[k : k + 1, :].astype(F32), 0.0)
    eye = (
        lax.broadcasted_iota(jnp.int32, (128, 128), 0)
        == lax.broadcasted_iota(jnp.int32, (128, 128), 1)
    ).astype(BF)
    own_gates = dot(dense.astype(BF), eye, TN)
    xs[0, :, width:] = own_gates.astype(BF)

    def column(v, e):
        lane = lax.broadcasted_iota(jnp.int32, v.shape, 1)
        return jnp.sum(jnp.where(lane == e, v, 0.0), axis=1, keepdims=True)

    def before(hits):
        rows = hits.shape[0]
        r = lax.broadcasted_iota(jnp.int32, (rows, rows), 0)
        c = lax.broadcasted_iota(jnp.int32, (rows, rows), 1)
        earlier = jnp.logical_and(c < r, c // tok == r // tok).astype(BF)
        return dot(earlier, hits.astype(BF))

    own_hits = (own_gates > 0).astype(F32)
    own_rank = before(own_hits)
    lane = lax.broadcasted_iota(jnp.int32, (tok, count), 1).astype(F32)
    main_pick = [jnp.zeros((tok, count), F32) for _ in range(2)]
    rest_pick = [jnp.zeros((tok, count), F32) for _ in range(8)]
    for j in range(owners):
        e = z_peer(j)
        hit, rank = column(own_hits, e), column(own_rank, e)
        low = jnp.where(rank < 8, hit, 0.0)
        high = hit - low
        for h in range(2):
            main_pick[h] += jnp.where(lane == tok * j + 8 * h + rank, low, 0.0)
        for q in range(8):
            rest_pick[q] += jnp.where(lane == tok * j + 2 * q + rank - 8, high, 0.0)
    main_pick = jnp.concatenate(main_pick, axis=0).astype(BF)
    rest_pick = jnp.concatenate(rest_pick, axis=0).astype(BF)
    c = lax.broadcasted_iota(jnp.int32, (count, count), 1)
    perm = (
        lax.broadcasted_iota(jnp.int32, (count, count), 0)
        == 16 * ((c >> 1) & 3) + 2 * (c >> 3) + (c & 1)
    ).astype(BF)

    def fold(y, dst):
        for k in range(owners):
            rows = y[8 * k : 8 * k + 8]
            dst[k, :, :half] = jnp.concatenate([rows[:, :half], rows[:, half:]], axis=0).astype(BF)
        rest = jnp.concatenate(
            [y[32:40, eighth * j : eighth * (j + 1)] for j in range(8)], axis=0
        ).astype(BF)
        dst[:, :, half:] = dot(perm, rest).astype(BF).reshape(owners, tok, eighth)

    def unfold(src, dst):
        main = dot(main_pick, src[:, :, :half].reshape(count, half))
        rest = dot(rest_pick, src[:, :, half:].reshape(count, eighth))
        for q in range(8):
            h, at = q // 4, q % 4 * eighth
            dst[:, q * eighth : (q + 1) * eighth] = (
                main[tok * h : tok * (h + 1), at : at + eighth] + rest[tok * q : tok * (q + 1)]
            ).astype(BF)

    flag = swapped_ref[me]
    loads[0].wait()
    loads[1].wait()
    pl.semaphore_wait(barrier, owners + groups - 2)

    hops = ((2, me < 2), (-2, me > 1), (1, me < 3), (-1, me > 0))

    def gather(buf, s, r):
        for d, there in hops:
            slot = -d % owners

            @pl.when(there)
            def _():
                send(
                    buf.at[0], buf.at[slot], s, r + slot - 1, expert=lax.rem(me + d + owners, owners)
                ).start()

    def pass_on(buf, s, r):
        arrived(buf.at[2], r + 1)
        slot = 1 + 2 * lax.rem(me, 2)

        @pl.when(middle)
        def _():
            pltpu.make_async_remote_copy(
                src_ref=buf.at[2],
                dst_ref=buf.at[slot],
                send_sem=left.at[s],
                recv_sem=came.at[r + slot - 1],
                device_id={"expert": lax.rem(3 * (me + 3), owners)},
                device_id_type=pl.DeviceIdType.MESH,
            ).start()

    def spread(buf, dst, at, s, r):
        for f in range(1, groups):
            p = peer(f)
            send(buf.at[at, :, cols(p)], dst.at[back(f), at], s, r, dp=p).start()
        dst[0, at] = buf[at, :, cols(group)]

    rest = pl.ds(1, owners - 1)

    def spread_rest(buf, dst, s, r):
        for f in range(1, groups):
            p = peer(f)
            send(buf.at[rest, :, cols(p)], dst.at[back(f), rest], s, r, dp=p).start()
        dst[0, 1:] = buf[1:, :, cols(group)]

    gather(xs, S_X, X_IN)
    gather(ogs, S_OG, OG_IN)
    spread(xs, x_in, 0, S_X_OWN, X_OWN)
    spread(ogs, og_in, 0, S_OG_OWN, OG_OWN)
    pass_on(xs, S_X, X_IN)
    arrived(xs.at[1], X_IN)
    arrived(xs.at[3], X_IN + 2)
    spread_rest(xs, x_in, S_X_REST, X_REST)
    pass_on(ogs, S_OG, OG_IN)

    gates = xs[:, :, width:].reshape(count, 128).astype(F32)
    gate = column(gates, me)
    hits = (gates > 0).astype(F32)
    hit, rank = column(hits, me), column(before(hits), me)
    block = (lax.broadcasted_iota(jnp.int32, (count, 1), 0) // tok).astype(F32)
    row = jnp.where(rank < 8, 8 * block + rank, 32 + 2 * block + rank - 8)
    lane = lax.broadcasted_iota(jnp.int32, (count, 48), 1).astype(F32)
    pack = jnp.where(lane == row, hit, 0.0).astype(BF)

    loads[2].wait()
    up = up_buf[...]
    hidden = dot(xs[:, :, :width].reshape(count, width), up)
    sigma = 1.0 / (1.0 + jnp.exp(-hidden))
    active = (gate * (hidden * sigma)).astype(BF)
    slope = sigma * (1.0 + hidden * (1.0 - sigma))
    own_act[...] = active
    partner = lax.rem(me + 2, owners)
    send(own_act, other_act, S_SWAP_ACT, SWAP_ACT, expert=partner).start()
    loads[3].wait()
    down = down_buf[...]
    fold(dot(dot(pack, active, TN).astype(BF), down), y_out)

    arrived(ogs.at[1], OG_IN)
    arrived(ogs.at[3], OG_IN + 2)
    spread_rest(ogs, og_in, S_OG_REST, OG_REST)
    dy = (gate * ogs[...].reshape(count, width).astype(F32)).astype(BF)
    d_hidden = (dot(dy, down, NT) * slope).astype(BF)
    own_dh[...] = d_hidden
    send(own_dh, other_dh, S_SWAP_DH, SWAP_DH, expert=partner).start()

    def send_back(out, into, s, r):
        for k in (2, 1, 3):
            send(out.at[k], into.at[owners - k], s, r, expert=z_peer(k)).start()
        into[0] = out[0]

    send_back(y_out, y_in, S_Y, Y)

    def choose(other, own, dst):
        turned = jnp.concatenate([other[count // 2 :], other[: count // 2]], axis=0)
        dst[0] = jnp.where(flag == 1, turned, own[...])

    def tell(buf, s, r, r_twin):
        for i in (2, 1, 3):
            send(buf.at[0], buf.at[4 - i], s, r + 3 - i, dp=peer(i)).start()
        send(buf.at[0], buf.at[4], s, r_twin, dp=twin).start()

    def retell(buf, s, r, r_twin):
        for i in (1, 2, 3):
            arrived(buf.at[i], r + i - 1)
            send(buf.at[i], buf.at[4 + i], s, r_twin, dp=twin).start()

    arrived(other_act, SWAP_ACT)
    choose(other_act, own_act, act_all)
    tell(act_all, S_ACT, ACT_IN, ACT_TWIN)

    fold(dot(dot(pack, d_hidden, TN).astype(BF), up, NT), dx_out)
    send_back(dx_out, dx_in, S_DX, DX)

    arrived(other_dh, SWAP_DH)
    choose(other_dh, own_dh, dh_all)
    tell(dh_all, S_DH, DH_IN, DH_TWIN)
    retell(act_all, S_ACT, ACT_IN, ACT_TWIN)

    total = groups * count
    others = pl.ds(1, groups - 1)
    arrived(og_in.at[others, 0], OG_OWN)
    arrived(og_in.at[others, rest], OG_REST)
    arrived(act_all.at[pl.ds(4, 4)], ACT_TWIN)
    down_out[...] = (
        dot(act_all[...].reshape(total, fw), og_in[...].reshape(total, part), TN)
        .astype(BF)
        .reshape(groups, depth, part)
    )
    for f in range(1, groups):
        p = peer(f)
        send(down_out.at[p], down_in.at[back(f)], S_DOWN, DOWN, dp=p).start()
    down_in[0] = down_out[group]
    retell(dh_all, S_DH, DH_IN, DH_TWIN)
    arrived(x_in.at[others, 0], X_OWN)
    arrived(x_in.at[others, rest], X_REST)
    arrived(dh_all.at[pl.ds(4, 4)], DH_TWIN)
    ugrad_ref[0] = dot(x_in[...].reshape(total, part), dh_all[...].reshape(total, fw), TN)

    arrived(y_in.at[rest], Y)
    unfold(y_in, out_ref)
    arrived(down_in.at[others], DOWN)
    for f in range(groups):
        dgrad_ref[0, :, cols(peer(f))] = down_in[f].astype(F32)
    arrived(dx_in.at[rest], DX)
    unfold(dx_in, tgrad_ref)

    for buf, s in ((xs, S_X), (ogs, S_OG)):

        @pl.when(middle)
        def _():
            departed(buf, s)

        @pl.when(jnp.logical_not(middle))
        def _():
            departed(buf.at[pl.ds(0, 2)], s)

    departed(x_in.at[others, 0], S_X_OWN)
    departed(og_in.at[others, 0], S_OG_OWN)
    departed(x_in.at[others, rest], S_X_REST)
    departed(og_in.at[others, rest], S_OG_REST)
    departed(own_act, S_SWAP_ACT)
    departed(own_dh, S_SWAP_DH)
    departed(act_all.at[others], S_ACT)
    departed(dh_all.at[others], S_DH)
    departed(down_in.at[others], S_DOWN)
    departed(y_in.at[rest], S_Y)
    departed(dx_in.at[rest], S_DX)


def place(*refs):
    count = (len(refs) - 1) // 2
    copies = [
        pltpu.make_async_copy(refs[i], refs[count + i], refs[-1].at[i]) for i in range(count)
    ]
    for copy in copies:
        copy.start()
    for copy in copies:
        copy.wait()


def by_kernel(groups, owners, tokens, out_grad, gate_weights, expert_ids, swapped, up, down):
    tok, width = tokens.shape
    fw = up.shape[2]
    part, depth, count = width // groups, fw // groups, owners * tok
    vmem = pl.BlockSpec(memory_space=pltpu.VMEM)
    hbm = pl.BlockSpec(memory_space=pltpu.HBM)
    dma = pltpu.SemaphoreType.DMA
    shapes = (
        ((tok, width), BF),
        ((tok, width), BF),
        ((1, part, fw), F32),
        ((1, depth, width), F32),
    )
    cut = pltpu.VMEM((groups, owners, tok, part), BF)
    hid = pltpu.VMEM((count, fw), BF)
    every = pltpu.VMEM((groups, count, fw), BF)
    folded = pltpu.VMEM((owners, tok, width // 2 + width // 8), BF)
    block = pltpu.VMEM((groups, depth, part), BF)
    params = pltpu.CompilerParams(
        collective_id=0, has_side_effects=True, vmem_limit_bytes=62 << 20
    )
    results = pl.pallas_call(
        kernel,
        out_shape=tuple(pltpu.VMEM(*a) for a in shapes),
        in_specs=[pl.BlockSpec(memory_space=pltpu.SMEM), hbm, hbm, vmem, vmem, hbm, hbm],
        out_specs=(vmem,) * 4,
        scratch_shapes=[
            pltpu.VMEM((owners, tok, width + 128), BF),
            pltpu.VMEM((owners, tok, width), BF),
            pltpu.VMEM(up.shape[1:], BF),
            pltpu.VMEM(down.shape[1:], BF),
            cut,
            cut,
            hid,
            hid,
            hid,
            hid,
            every,
            every,
            folded,
            folded,
            folded,
            folded,
            block,
            block,
            dma((4,)),
            dma((DEPARTURES,)),
            dma((ARRIVALS,)),
        ],
        compiler_params=params,
    )(swapped, tokens, out_grad, gate_weights.T, expert_ids.T, up, down)
    return pl.pallas_call(
        place,
        out_shape=tuple(jax.ShapeDtypeStruct(*a) for a in shapes),
        in_specs=[vmem] * 4,
        out_specs=(hbm,) * 4,
        scratch_shapes=[dma((4,))],
        compiler_params=pltpu.CompilerParams(vmem_limit_bytes=40 << 20),
    )(*results)


def solution(mesh):
    groups, owners = mesh.shape["dp"], mesh.shape["expert"]

    def on_device(tokens, out_grad, gate_weights, expert_ids, swapped, up_weight, down_weight):
        args = (tokens, out_grad, gate_weights, expert_ids, swapped, up_weight, down_weight)
        tok, width = tokens.shape
        fw = up_weight.shape[2]
        known = (groups, owners, tok, expert_ids.shape[1]) == (8, 4, 16, 2)
        if known and width % (128 * groups) == 0 and fw % (16 * groups) == 0:
            return by_kernel(groups, owners, *args)
        return by_collectives(*args)

    rows = P(("dp", "expert"), None)
    in_specs = (rows, rows, rows, rows, P(), P("expert", None, None), P("expert", None, None))
    out_specs = (rows, rows, P("expert", "dp", None), P("expert", "dp", None))
    return jax.shard_map(
        on_device, mesh=mesh, in_specs=in_specs, out_specs=out_specs, check_vma=False
    )
```

time: 39.5 us -> 32.7 us (0.83)
  Pallas kernels: 38.7 us -> 31.9 us
    pallas_call x2, Pallas kernels: 38.7 us -> 31.9 us  [the longest x1 30.9 us: by_kernel(): pl.pallas_call(kernel, out_shape=tuple((pltpu.VMEM(*a) for a in shapes)),...]
where the time goes in v1:
time: 32.7 us; the launch traced here: 32.5 us
  Pallas kernels  31.9 us (98%)
  between operations  0.64 us (2%)
    pallas_call x1, Pallas kernels, by_kernel(): pl.pallas_call(kernel, out_shape=tuple((pltpu.VMEM(*a) for a in shapes)),...  30.9 us
    pallas_call x1, Pallas kernels, by_kernel(): pl.pallas_call(place, out_shape=tuple((jax.ShapeDtypeStruct(*a) for a in...  0.96 us

profile of v1, /device:TPU:0, one launch (start us, length us, event | category | flops | bytes accessed | tf_op | source)
XLA Modules:
  0.0 32.5 jit_solution(1001477577277177950)
XLA Ops:
  0.6 30.9 %shard_map.102 = (bf16[16,2048]{1,0:T(8,128)(2,1)S(1)}, bf16[16,2048]{1,0:T(8,128)(2,1)S(1)}, f32[1,256,384]{2,1,0:T(8,128)S(1)}, f32[1,48,2048]{2,1,0:T(8,128)S(1)}) custom-call(s32[4]{0:T(128)} %swapped_ref.1, bf16[16,2048]{1,0:T(8,128)(2,1)} %tok_ref.1, bf16[16,2048]{1,0:T(8,128)(2,1)} %og_ref.1, bf16[2,16]{1,0:T(2,128)(2,1)} %bitcast.3, ...), custom_call_target="tpu_custom_call" | custom-call | tf_op jit(solution)/shard_map/pallas_call | solution.py:444
  31.6 1.0 %shard_map.103 = (bf16[16,2048]{1,0:T(8,128)(2,1)}, bf16[16,2048]{1,0:T(8,128)(2,1)}, f32[1,256,384]{2,1,0:T(8,128)}, f32[1,48,2048]{2,1,0:T(8,128)}) custom-call(bf16[16,2048]{1,0:T(8,128)(2,1)S(1)} %get-tuple-element.8.refs_0_, bf16[16,2048]{1,0:T(8,128)(2,1)S(1)} %get-tuple-element.9.refs_1_, f32[1,256,384]{2,1,0:T(8,128)S(1)} %get-tuple-element.10.refs_2_, ...), custom_call_target="tpu_custom_call" | custom-call | tf_op jit(solution)/shard_map/pallas_call | solution.py:474

commit v2 on v1

--- a/solution.py
+++ b/solution.py
@@ -65,33 +65,22 @@
     return lax.dot_general(a, b, dims, preferred_element_type=F32)
 
 
-X_IN, OG_IN, X_OWN, OG_OWN, X_REST, OG_REST = 0, 3, 6, 7, 8, 9
-SWAP_ACT, SWAP_DH, ACT_IN, ACT_TWIN, DH_IN, DH_TWIN, DOWN, Y, DX = 10, 11, 12, 15, 16, 19, 20, 21, 22
-ARRIVALS = 23
-(
-    S_X,
-    S_OG,
-    S_X_OWN,
-    S_OG_OWN,
-    S_X_REST,
-    S_OG_REST,
-    S_SWAP_ACT,
-    S_SWAP_DH,
-    S_ACT,
-    S_DH,
-    S_DOWN,
-    S_Y,
-    S_DX,
-) = range(13)
-DEPARTURES = 13
+X_OWN, OG_OWN, X_REST, OG_REST, SWAP_ACT, SWAP_DH = range(6)
+ACT_IN, ACT_TWIN, DH_IN, DH_TWIN, DOWN, Y, DX, GATES = 6, 9, 10, 13, 14, 15, 16, 17
+X_IN, OG_IN = 18, 21
+GATES_ALL = 24
+ARRIVALS = 25
+S_X, S_OG, S_X_ON, S_OG_ON, S_X_OWN, S_OG_OWN, S_X_REST, S_OG_REST = range(8)
+S_SWAP_ACT, S_SWAP_DH, S_ACT, S_DH, S_DOWN, S_Y, S_DX, S_GATES, S_GATES_ALL = range(8, 17)
+DEPARTURES = 17
 
 
 def kernel(
-    swapped_ref,
+    swapped_hbm,
     tok_ref,
     og_ref,
-    gate_ref,
-    ids_ref,
+    gate_hbm,
+    ids_hbm,
     up_ref,
     down_ref,
     out_ref,
@@ -100,6 +89,10 @@
     dgrad_ref,
     xs,
     ogs,
+    gs,
+    gs_all,
+    x_rows,
+    og_rows,
     up_buf,
     down_buf,
     x_in,
@@ -116,6 +109,9 @@
     dx_in,
     down_out,
     down_in,
+    swapped_ref,
+    gate_ref,
+    ids_ref,
     load,
     left,
     came,
@@ -125,6 +121,7 @@
     fw = up_ref.shape[2]
     part, depth, half, eighth = width // groups, fw // groups, width // 2, width // 8
     count = owners * tok
+    room = own_act.shape[0]
     me = lax.axis_index("expert")
     group = lax.axis_index("dp")
     chip, core = group // 2, lax.rem(group, 2)
@@ -168,14 +165,23 @@
         pl.semaphore_signal(
             barrier, inc=1, device_id={"dp": peer(f)}, device_id_type=pl.DeviceIdType.MESH
         )
+    small = [
+        pltpu.make_async_copy(ids_hbm, ids_ref, load.at[4]),
+        pltpu.make_async_copy(gate_hbm, gate_ref, load.at[5]),
+        pltpu.make_async_copy(swapped_hbm, swapped_ref, load.at[6]),
+    ]
+    for copy in small:
+        copy.start()
     loads = [
-        pltpu.make_async_copy(tok_ref, xs.at[0, :, pl.ds(0, width)], load.at[0]),
+        pltpu.make_async_copy(tok_ref, xs.at[0], load.at[0]),
         pltpu.make_async_copy(og_ref, ogs.at[0], load.at[1]),
         pltpu.make_async_copy(up_ref.at[0], up_buf, load.at[2]),
         pltpu.make_async_copy(down_ref.at[0], down_buf, load.at[3]),
     ]
     for copy in loads:
         copy.start()
+    for copy in small:
+        copy.wait()
     lines = lax.broadcasted_iota(jnp.int32, (128, tok), 0)
     dense = jnp.zeros((128, tok), F32)
     for k in range(ids_ref.shape[0]):
@@ -186,7 +192,7 @@
         == lax.broadcasted_iota(jnp.int32, (128, 128), 1)
     ).astype(BF)
     own_gates = dot(dense.astype(BF), eye, TN)
-    xs[0, :, width:] = own_gates.astype(BF)
+    gs[0] = own_gates.astype(BF)
 
     def column(v, e):
         lane = lax.broadcasted_iota(jnp.int32, v.shape, 1)
@@ -199,27 +205,17 @@
         earlier = jnp.logical_and(c < r, c // tok == r // tok).astype(BF)
         return dot(earlier, hits.astype(BF))
 
-    own_hits = (own_gates > 0).astype(F32)
-    own_rank = before(own_hits)
-    lane = lax.broadcasted_iota(jnp.int32, (tok, count), 1).astype(F32)
-    main_pick = [jnp.zeros((tok, count), F32) for _ in range(2)]
-    rest_pick = [jnp.zeros((tok, count), F32) for _ in range(8)]
-    for j in range(owners):
-        e = z_peer(j)
-        hit, rank = column(own_hits, e), column(own_rank, e)
-        low = jnp.where(rank < 8, hit, 0.0)
-        high = hit - low
-        for h in range(2):
-            main_pick[h] += jnp.where(lane == tok * j + 8 * h + rank, low, 0.0)
-        for q in range(8):
-            rest_pick[q] += jnp.where(lane == tok * j + 2 * q + rank - 8, high, 0.0)
-    main_pick = jnp.concatenate(main_pick, axis=0).astype(BF)
-    rest_pick = jnp.concatenate(rest_pick, axis=0).astype(BF)
-    c = lax.broadcasted_iota(jnp.int32, (count, count), 1)
-    perm = (
-        lax.broadcasted_iota(jnp.int32, (count, count), 0)
-        == 16 * ((c >> 1) & 3) + 2 * (c >> 3) + (c & 1)
-    ).astype(BF)
+    def named(gates, e, lanes):
+        pick = lax.broadcasted_iota(jnp.int32, (128, lanes), 0) == e
+        return (dot(gates, pick.astype(BF)) > 0).astype(F32)
+
+    def packing(hits, turn):
+        rank = before(hits)
+        block = lax.broadcasted_iota(jnp.int32, hits.shape, 0) // tok
+        block = ((block + turn) & 3).astype(F32)
+        row = jnp.where(rank < 8, 8 * block + rank, 32 + 2 * block + rank - 8)
+        lane = lax.broadcasted_iota(jnp.int32, hits.shape, 1).astype(F32)
+        return jnp.where(lane == row, hits, 0.0).astype(BF)
 
     def fold(y, dst):
         for k in range(owners):
@@ -240,20 +236,16 @@
             ).astype(BF)
 
     flag = swapped_ref[me]
-    loads[0].wait()
-    loads[1].wait()
     pl.semaphore_wait(barrier, owners + groups - 2)
 
-    hops = ((2, me < 2), (-2, me > 1), (1, me < 3), (-1, me > 0))
-
-    def gather(buf, s, r):
-        for d, there in hops:
+    def gather(src, buf, s, r):
+        for d, there in ((2, me < 2), (-2, me > 1), (1, me < 3), (-1, me > 0)):
             slot = -d % owners
 
             @pl.when(there)
             def _():
                 send(
-                    buf.at[0], buf.at[slot], s, r + slot - 1, expert=lax.rem(me + d + owners, owners)
+                    src, buf.at[slot], s, r + slot - 1, expert=lax.rem(me + d + owners, owners)
                 ).start()
 
     def pass_on(buf, s, r):
@@ -271,11 +263,10 @@
                 device_id_type=pl.DeviceIdType.MESH,
             ).start()
 
-    def spread(buf, dst, at, s, r):
+    def spread_own(src, dst, s, r):
         for f in range(1, groups):
             p = peer(f)
-            send(buf.at[at, :, cols(p)], dst.at[back(f), at], s, r, dp=p).start()
-        dst[0, at] = buf[at, :, cols(group)]
+            send(src.at[:, cols(p)], dst.at[back(f), 0], s, r, dp=p).start()
 
     rest = pl.ds(1, owners - 1)
 
@@ -285,44 +276,65 @@
             send(buf.at[rest, :, cols(p)], dst.at[back(f), rest], s, r, dp=p).start()
         dst[0, 1:] = buf[1:, :, cols(group)]
 
-    gather(xs, S_X, X_IN)
-    gather(ogs, S_OG, OG_IN)
-    spread(xs, x_in, 0, S_X_OWN, X_OWN)
-    spread(ogs, og_in, 0, S_OG_OWN, OG_OWN)
-    pass_on(xs, S_X, X_IN)
+    for k in (2, 1, 3):
+        send(gs.at[0], gs.at[owners - k], S_GATES, GATES, expert=z_peer(k)).start()
+    gather(tok_ref, xs, S_X, X_IN)
+    gather(og_ref, ogs, S_OG, OG_IN)
+    spread_own(tok_ref, x_in, S_X_OWN, X_OWN)
+    spread_own(og_ref, og_in, S_OG_OWN, OG_OWN)
+    pass_on(xs, S_X_ON, X_IN)
     arrived(xs.at[1], X_IN)
     arrived(xs.at[3], X_IN + 2)
+    loads[0].wait()
+    x_in[0, 0] = xs[0, :, cols(group)]
     spread_rest(xs, x_in, S_X_REST, X_REST)
-    pass_on(ogs, S_OG, OG_IN)
-
-    gates = xs[:, :, width:].reshape(count, 128).astype(F32)
-    gate = column(gates, me)
-    hits = (gates > 0).astype(F32)
-    hit, rank = column(hits, me), column(before(hits), me)
-    block = (lax.broadcasted_iota(jnp.int32, (count, 1), 0) // tok).astype(F32)
-    row = jnp.where(rank < 8, 8 * block + rank, 32 + 2 * block + rank - 8)
-    lane = lax.broadcasted_iota(jnp.int32, (count, 48), 1).astype(F32)
-    pack = jnp.where(lane == row, hit, 0.0).astype(BF)
+    pass_on(ogs, S_OG_ON, OG_IN)
+
+    arrived(gs.at[rest], GATES)
+    for f in range(1, groups):
+        send(gs, gs_all.at[back(f)], S_GATES_ALL, GATES_ALL, dp=peer(f)).start()
+    gs_all[0] = gs[...]
+    gates = gs[...].reshape(count, 128)
+    gate = column(gates.astype(F32), me)
+    pack = packing(named(gates, me, room), 0)
 
     loads[2].wait()
     up = up_buf[...]
-    hidden = dot(xs[:, :, :width].reshape(count, width), up)
+    hidden = dot(xs[...].reshape(count, width), up)
     sigma = 1.0 / (1.0 + jnp.exp(-hidden))
     active = (gate * (hidden * sigma)).astype(BF)
     slope = sigma * (1.0 + hidden * (1.0 - sigma))
-    own_act[...] = active
+    own_act[...] = dot(pack, active, TN).astype(BF)
     partner = lax.rem(me + 2, owners)
     send(own_act, other_act, S_SWAP_ACT, SWAP_ACT, expert=partner).start()
+    spot = lax.broadcasted_iota(jnp.int32, (1, count), 1)
+    own_hits = named(own_gates.astype(BF), (me + spot // tok) & 3, count)
+    own_rank = before(own_hits)
+    spot = (spot & (tok - 1)).astype(F32)
+    low = jnp.where(own_rank < 8, own_hits, 0.0)
+    high = own_hits - low
+    main_pick = [jnp.where(spot == 8 * h + own_rank, low, 0.0) for h in range(2)]
+    rest_pick = [jnp.where(spot == 2 * q + own_rank - 8, high, 0.0) for q in range(8)]
+    main_pick = jnp.concatenate(main_pick, axis=0).astype(BF)
+    rest_pick = jnp.concatenate(rest_pick, axis=0).astype(BF)
+    c = lax.broadcasted_iota(jnp.int32, (count, count), 1)
+    perm = (
+        lax.broadcasted_iota(jnp.int32, (count, count), 0)
+        == 16 * ((c >> 1) & 3) + 2 * (c >> 3) + (c & 1)
+    ).astype(BF)
+
     loads[3].wait()
     down = down_buf[...]
-    fold(dot(dot(pack, active, TN).astype(BF), down), y_out)
+    fold(dot(own_act[...], down), y_out)
 
     arrived(ogs.at[1], OG_IN)
     arrived(ogs.at[3], OG_IN + 2)
+    loads[1].wait()
+    og_in[0, 0] = ogs[0, :, cols(group)]
     spread_rest(ogs, og_in, S_OG_REST, OG_REST)
     dy = (gate * ogs[...].reshape(count, width).astype(F32)).astype(BF)
     d_hidden = (dot(dy, down, NT) * slope).astype(BF)
-    own_dh[...] = d_hidden
+    own_dh[...] = dot(pack, d_hidden, TN).astype(BF)
     send(own_dh, other_dh, S_SWAP_DH, SWAP_DH, expert=partner).start()
 
     def send_back(out, into, s, r):
@@ -330,11 +342,9 @@
             send(out.at[k], into.at[owners - k], s, r, expert=z_peer(k)).start()
         into[0] = out[0]
 
-    send_back(y_out, y_in, S_Y, Y)
 
     def choose(other, own, dst):
-        turned = jnp.concatenate([other[count // 2 :], other[: count // 2]], axis=0)
-        dst[0] = jnp.where(flag == 1, turned, own[...])
+        dst[0] = jnp.where(flag == 1, other[...], own[...])
 
     def tell(buf, s, r, r_twin):
         for i in (2, 1, 3):
@@ -349,22 +359,35 @@
     arrived(other_act, SWAP_ACT)
     choose(other_act, own_act, act_all)
     tell(act_all, S_ACT, ACT_IN, ACT_TWIN)
-
-    fold(dot(dot(pack, d_hidden, TN).astype(BF), up, NT), dx_out)
-    send_back(dx_out, dx_in, S_DX, DX)
+    send_back(y_out, y_in, S_Y, Y)
+
+    fold(dot(own_dh[...], up, NT), dx_out)
+
+    held = jnp.where(flag == 1, partner, me)
+    others = pl.ds(1, groups - 1)
+    arrived(gs_all.at[others], GATES_ALL)
+    turn = jnp.where(flag == 1, 2, 0)
+    hits = named(gs_all[...].reshape(groups * count, 128), held, room)
+    packs = [packing(hits[count * f : count * (f + 1)], turn) for f in range(groups)]
+    arrived(x_in.at[others, 0], X_OWN)
+    arrived(x_in.at[others, rest], X_REST)
+    for f in range(groups):
+        x_rows[f] = dot(packs[f], x_in[f].reshape(count, part), TN).astype(BF)
 
     arrived(other_dh, SWAP_DH)
     choose(other_dh, own_dh, dh_all)
     tell(dh_all, S_DH, DH_IN, DH_TWIN)
+    send_back(dx_out, dx_in, S_DX, DX)
     retell(act_all, S_ACT, ACT_IN, ACT_TWIN)
 
-    total = groups * count
-    others = pl.ds(1, groups - 1)
+    total = groups * room
     arrived(og_in.at[others, 0], OG_OWN)
     arrived(og_in.at[others, rest], OG_REST)
+    for f in range(groups):
+        og_rows[f] = dot(packs[f], og_in[f].reshape(count, part), TN).astype(BF)
     arrived(act_all.at[pl.ds(4, 4)], ACT_TWIN)
     down_out[...] = (
-        dot(act_all[...].reshape(total, fw), og_in[...].reshape(total, part), TN)
+        dot(act_all[...].reshape(total, fw), og_rows[...].reshape(total, part), TN)
         .astype(BF)
         .reshape(groups, depth, part)
     )
@@ -373,10 +396,8 @@
         send(down_out.at[p], down_in.at[back(f)], S_DOWN, DOWN, dp=p).start()
     down_in[0] = down_out[group]
     retell(dh_all, S_DH, DH_IN, DH_TWIN)
-    arrived(x_in.at[others, 0], X_OWN)
-    arrived(x_in.at[others, rest], X_REST)
     arrived(dh_all.at[pl.ds(4, 4)], DH_TWIN)
-    ugrad_ref[0] = dot(x_in[...].reshape(total, part), dh_all[...].reshape(total, fw), TN)
+    ugrad_ref[0] = dot(x_rows[...].reshape(total, part), dh_all[...].reshape(total, fw), TN)
 
     arrived(y_in.at[rest], Y)
     unfold(y_in, out_ref)
@@ -386,16 +407,19 @@
     arrived(dx_in.at[rest], DX)
     unfold(dx_in, tgrad_ref)
 
-    for buf, s in ((xs, S_X), (ogs, S_OG)):
+    for buf, s, s_on in ((xs, S_X, S_X_ON), (ogs, S_OG, S_OG_ON)):
 
         @pl.when(middle)
         def _():
-            departed(buf, s)
+            departed(buf.at[rest], s)
+            departed(buf.at[0], s_on)
 
         @pl.when(jnp.logical_not(middle))
         def _():
             departed(buf.at[pl.ds(0, 2)], s)
 
+    departed(gs.at[rest], S_GATES)
+    departed(gs_all.at[others], S_GATES_ALL)
     departed(x_in.at[others, 0], S_X_OWN)
     departed(og_in.at[others, 0], S_OG_OWN)
     departed(x_in.at[others, rest], S_X_REST)
@@ -434,8 +458,9 @@
         ((1, depth, width), F32),
     )
     cut = pltpu.VMEM((groups, owners, tok, part), BF)
-    hid = pltpu.VMEM((count, fw), BF)
-    every = pltpu.VMEM((groups, count, fw), BF)
+    room = 48
+    hid = pltpu.VMEM((room, fw), BF)
+    every = pltpu.VMEM((groups, room, fw), BF)
     folded = pltpu.VMEM((owners, tok, width // 2 + width // 8), BF)
     block = pltpu.VMEM((groups, depth, part), BF)
     params = pltpu.CompilerParams(
@@ -444,11 +469,15 @@
     results = pl.pallas_call(
         kernel,
         out_shape=tuple(pltpu.VMEM(*a) for a in shapes),
-        in_specs=[pl.BlockSpec(memory_space=pltpu.SMEM), hbm, hbm, vmem, vmem, hbm, hbm],
+        in_specs=[hbm] * 7,
         out_specs=(vmem,) * 4,
         scratch_shapes=[
-            pltpu.VMEM((owners, tok, width + 128), BF),
             pltpu.VMEM((owners, tok, width), BF),
+            pltpu.VMEM((owners, tok, width), BF),
+            pltpu.VMEM((owners, tok, 128), BF),
+            pltpu.VMEM((groups, owners, tok, 128), BF),
+            pltpu.VMEM((groups, room, part), BF),
+            pltpu.VMEM((groups, room, part), BF),
             pltpu.VMEM(up.shape[1:], BF),
             pltpu.VMEM(down.shape[1:], BF),
             cut,
@@ -465,7 +494,10 @@
             folded,
             block,
             block,
-            dma((4,)),
+            pltpu.SMEM(swapped.shape, swapped.dtype),
+            pltpu.VMEM(gate_weights.shape[::-1], BF),
+            pltpu.VMEM(expert_ids.shape[::-1], jnp.int32),
+            dma((7,)),
             dma((DEPARTURES,)),
             dma((ARRIVALS,)),
         ],

time: 32.7 us -> 30.9 us (0.945)
  Pallas kernels: 31.9 us -> 30.1 us
    pallas_call x1, Pallas kernels: 30.9 us -> 29.1 us  [by_kernel(): pl.pallas_call(kernel, out_shape=tuple((pltpu.VMEM(*a) for a in shapes)),...]
where the time goes in v2:
time: 30.9 us; the launch traced here: 30.7 us
  Pallas kernels  30.1 us (97%)
  between operations  0.64 us (2%)
    pallas_call x1, Pallas kernels, by_kernel(): pl.pallas_call(kernel, out_shape=tuple((pltpu.VMEM(*a) for a in shapes)),...  29.1 us
    pallas_call x1, Pallas kernels, by_kernel(): pl.pallas_call(place, out_shape=tuple((jax.ShapeDtypeStruct(*a) for a in...  0.96 us

profile of v2, /device:TPU:0, one launch (start us, length us, event | category | flops | bytes accessed | tf_op | source)
XLA Modules:
  0.0 30.7 jit_solution(12786308503552253672)
XLA Ops:
  0.6 29.1 %shard_map.102 = (bf16[16,2048]{1,0:T(8,128)(2,1)S(1)}, bf16[16,2048]{1,0:T(8,128)(2,1)S(1)}, f32[1,256,384]{2,1,0:T(8,128)S(1)}, f32[1,48,2048]{2,1,0:T(8,128)S(1)}) custom-call(s32[4]{0:T(128)} %swapped_hbm.1, bf16[16,2048]{1,0:T(8,128)(2,1)} %tok_ref.1, bf16[16,2048]{1,0:T(8,128)(2,1)} %og_ref.1, bf16[2,16]{1,0:T(2,128)(2,1)} %bitcast.3, ...), custom_call_target="tpu_custom_call" | custom-call | tf_op jit(solution)/shard_map/pallas_call | solution.py:469
  29.8 1.0 %shard_map.103 = (bf16[16,2048]{1,0:T(8,128)(2,1)}, bf16[16,2048]{1,0:T(8,128)(2,1)}, f32[1,256,384]{2,1,0:T(8,128)}, f32[1,48,2048]{2,1,0:T(8,128)}) custom-call(bf16[16,2048]{1,0:T(8,128)(2,1)S(1)} %get-tuple-element.8.refs_0_, bf16[16,2048]{1,0:T(8,128)(2,1)S(1)} %get-tuple-element.9.refs_1_, f32[1,256,384]{2,1,0:T(8,128)S(1)} %get-tuple-element.10.refs_2_, ...), custom_call_target="tpu_custom_call" | custom-call | tf_op jit(solution)/shard_map/pallas_call | solution.py:506

commit v3 on v2

--- a/solution.py
+++ b/solution.py
@@ -95,6 +95,8 @@
     og_rows,
     up_buf,
     down_buf,
+    up_turned,
+    down_turned,
     x_in,
     og_in,
     own_act,
@@ -282,6 +284,8 @@
     gather(og_ref, ogs, S_OG, OG_IN)
     spread_own(tok_ref, x_in, S_X_OWN, X_OWN)
     spread_own(og_ref, og_in, S_OG_OWN, OG_OWN)
+    loads[3].wait()
+    down_turned[...] = down_buf[...].T
     pass_on(xs, S_X_ON, X_IN)
     arrived(xs.at[1], X_IN)
     arrived(xs.at[3], X_IN + 2)
@@ -323,23 +327,30 @@
         == 16 * ((c >> 1) & 3) + 2 * (c >> 3) + (c & 1)
     ).astype(BF)
 
-    loads[3].wait()
     down = down_buf[...]
     fold(dot(own_act[...], down), y_out)
 
+    up_turned[...] = up.T
     arrived(ogs.at[1], OG_IN)
     arrived(ogs.at[3], OG_IN + 2)
     loads[1].wait()
     og_in[0, 0] = ogs[0, :, cols(group)]
     spread_rest(ogs, og_in, S_OG_REST, OG_REST)
     dy = (gate * ogs[...].reshape(count, width).astype(F32)).astype(BF)
-    d_hidden = (dot(dy, down, NT) * slope).astype(BF)
+    d_hidden = (dot(dy, down_turned[...]) * slope).astype(BF)
     own_dh[...] = dot(pack, d_hidden, TN).astype(BF)
     send(own_dh, other_dh, S_SWAP_DH, SWAP_DH, expert=partner).start()
 
     def send_back(out, into, s, r):
-        for k in (2, 1, 3):
-            send(out.at[k], into.at[owners - k], s, r, expert=z_peer(k)).start()
+        for p in (0, 1, 2, 3):
+            k = lax.rem(p + owners - me, owners)
+
+            @pl.when(me != p)
+            def _():
+                send(
+                    out.at[k], into.at[lax.rem(me + owners - p, owners)], s, r, expert=p
+                ).start()
+
         into[0] = out[0]
 
 
@@ -361,7 +372,7 @@
     tell(act_all, S_ACT, ACT_IN, ACT_TWIN)
     send_back(y_out, y_in, S_Y, Y)
 
-    fold(dot(own_dh[...], up, NT), dx_out)
+    fold(dot(own_dh[...], up_turned[...]), dx_out)
 
     held = jnp.where(flag == 1, partner, me)
     others = pl.ds(1, groups - 1)
@@ -391,9 +402,13 @@
         .astype(BF)
         .reshape(groups, depth, part)
     )
-    for f in range(1, groups):
-        p = peer(f)
-        send(down_out.at[p], down_in.at[back(f)], S_DOWN, DOWN, dp=p).start()
+    for p in (0, 1, 2, 4, 6, 3, 5, 7):
+        b, i = lax.rem(p + core, 2), lax.rem(p // 2 + 4 - chip, 4)
+
+        @pl.when(group != p)
+        def _():
+            send(down_out.at[p], down_in.at[4 * b + lax.rem(4 - i, 4)], S_DOWN, DOWN, dp=p).start()
+
     down_in[0] = down_out[group]
     retell(dh_all, S_DH, DH_IN, DH_TWIN)
     arrived(dh_all.at[pl.ds(4, 4)], DH_TWIN)
@@ -435,9 +450,14 @@
 
 def place(*refs):
     count = (len(refs) - 1) // 2
-    copies = [
-        pltpu.make_async_copy(refs[i], refs[count + i], refs[-1].at[i]) for i in range(count)
-    ]
+    copies = []
+    for i in range(count):
+        for j in range(2):
+            rows = refs[i].shape[-2] // 2
+            at = (0,) * (len(refs[i].shape) - 2) + (pl.ds(j * rows, rows),)
+            copies.append(
+                pltpu.make_async_copy(refs[i].at[at], refs[count + i].at[at], refs[-1].at[2 * i + j])
+            )
     for copy in copies:
         copy.start()
     for copy in copies:
@@ -480,6 +500,8 @@
             pltpu.VMEM((groups, room, part), BF),
             pltpu.VMEM(up.shape[1:], BF),
             pltpu.VMEM(down.shape[1:], BF),
+            pltpu.VMEM(up.shape[:0:-1], BF),
+            pltpu.VMEM(down.shape[:0:-1], BF),
             cut,
             cut,
             hid,
@@ -508,7 +530,7 @@
         out_shape=tuple(jax.ShapeDtypeStruct(*a) for a in shapes),
         in_specs=[vmem] * 4,
         out_specs=(hbm,) * 4,
-        scratch_shapes=[dma((4,))],
+        scratch_shapes=[dma((8,))],
         compiler_params=pltpu.CompilerParams(vmem_limit_bytes=40 << 20),
     )(*results)
 

time: 30.9 us -> 30 us (0.971)
  Pallas kernels: 30.1 us -> 29.2 us
    pallas_call x1, Pallas kernels: 29.1 us -> 28.2 us  [by_kernel(): pl.pallas_call(kernel, out_shape=tuple((pltpu.VMEM(*a) for a in shapes)),...]
where the time goes in v3:
time: 30 us; the launch traced here: 29.8 us
  Pallas kernels  29.2 us (97%)
  between operations  0.64 us (2%)
    pallas_call x1, Pallas kernels, by_kernel(): pl.pallas_call(kernel, out_shape=tuple((pltpu.VMEM(*a) for a in shapes)),...  28.2 us
    pallas_call x1, Pallas kernels, by_kernel(): pl.pallas_call(place, out_shape=tuple((jax.ShapeDtypeStruct(*a) for a in...  0.99 us

profile of v3, /device:TPU:0, one launch (start us, length us, event | category | flops | bytes accessed | tf_op | source)
XLA Modules:
  0.0 29.8 jit_solution(7734493765533038664)
XLA Ops:
  0.6 28.2 %shard_map.102 = (bf16[16,2048]{1,0:T(8,128)(2,1)S(1)}, bf16[16,2048]{1,0:T(8,128)(2,1)S(1)}, f32[1,256,384]{2,1,0:T(8,128)S(1)}, f32[1,48,2048]{2,1,0:T(8,128)S(1)}) custom-call(s32[4]{0:T(128)} %swapped_hbm.1, bf16[16,2048]{1,0:T(8,128)(2,1)} %tok_ref.1, bf16[16,2048]{1,0:T(8,128)(2,1)} %og_ref.1, bf16[2,16]{1,0:T(2,128)(2,1)} %bitcast.3, ...), custom_call_target="tpu_custom_call" | custom-call | tf_op jit(solution)/shard_map/pallas_call | solution.py:489
  28.8 1.0 %shard_map.103 = (bf16[16,2048]{1,0:T(8,128)(2,1)}, bf16[16,2048]{1,0:T(8,128)(2,1)}, f32[1,256,384]{2,1,0:T(8,128)}, f32[1,48,2048]{2,1,0:T(8,128)}) custom-call(bf16[16,2048]{1,0:T(8,128)(2,1)S(1)} %get-tuple-element.8.refs_0_, bf16[16,2048]{1,0:T(8,128)(2,1)S(1)} %get-tuple-element.9.refs_1_, f32[1,256,384]{2,1,0:T(8,128)S(1)} %get-tuple-element.10.refs_2_, ...), custom_call_target="tpu_custom_call" | custom-call | tf_op jit(solution)/shard_map/pallas_call | solution.py:528

commit v4 on v3

--- a/solution.py
+++ b/solution.py
@@ -358,8 +358,14 @@
         dst[0] = jnp.where(flag == 1, other[...], own[...])
 
     def tell(buf, s, r, r_twin):
-        for i in (2, 1, 3):
-            send(buf.at[0], buf.at[4 - i], s, r + 3 - i, dp=peer(i)).start()
+        for to in range(4):
+            slot = lax.rem(chip + 4 - to, 4)
+
+            @pl.when(chip != to)
+            def _():
+                at = lax.rem(slot + 3, 4)
+                send(buf.at[0], buf.at[slot], s, r + at, dp=2 * to + core).start()
+
         send(buf.at[0], buf.at[4], s, r_twin, dp=twin).start()
 
     def retell(buf, s, r, r_twin):
@@ -402,7 +408,7 @@
         .astype(BF)
         .reshape(groups, depth, part)
     )
-    for p in (0, 1, 2, 4, 6, 3, 5, 7):
+    for p in (0, 1, 6, 4, 2, 7, 5, 3):
         b, i = lax.rem(p + core, 2), lax.rem(p // 2 + 4 - chip, 4)
 
         @pl.when(group != p)

time: 30 us -> 30 us (level)
  no operation moved by 1% of the time
where the time goes in v4:
time: 30 us; the launch traced here: 29.8 us
  Pallas kernels  29.2 us (97%)
  between operations  0.64 us (2%)
    pallas_call x1, Pallas kernels, by_kernel(): pl.pallas_call(kernel, out_shape=tuple((pltpu.VMEM(*a) for a in shapes)),...  28.2 us
    pallas_call x1, Pallas kernels, by_kernel(): pl.pallas_call(place, out_shape=tuple((jax.ShapeDtypeStruct(*a) for a in...  0.99 us

profile of v4, /device:TPU:0, one launch (start us, length us, event | category | flops | bytes accessed | tf_op | source)
XLA Modules:
  0.0 29.8 jit_solution(17072968480340951415)
XLA Ops:
  0.6 28.2 %shard_map.102 = (bf16[16,2048]{1,0:T(8,128)(2,1)S(1)}, bf16[16,2048]{1,0:T(8,128)(2,1)S(1)}, f32[1,256,384]{2,1,0:T(8,128)S(1)}, f32[1,48,2048]{2,1,0:T(8,128)S(1)}) custom-call(s32[4]{0:T(128)} %swapped_hbm.1, bf16[16,2048]{1,0:T(8,128)(2,1)} %tok_ref.1, bf16[16,2048]{1,0:T(8,128)(2,1)} %og_ref.1, bf16[2,16]{1,0:T(2,128)(2,1)} %bitcast.3, ...), custom_call_target="tpu_custom_call" | custom-call | tf_op jit(solution)/shard_map/pallas_call | solution.py:495
  28.8 1.0 %shard_map.103 = (bf16[16,2048]{1,0:T(8,128)(2,1)}, bf16[16,2048]{1,0:T(8,128)(2,1)}, f32[1,256,384]{2,1,0:T(8,128)}, f32[1,48,2048]{2,1,0:T(8,128)}) custom-call(bf16[16,2048]{1,0:T(8,128)(2,1)S(1)} %get-tuple-element.8.refs_0_, bf16[16,2048]{1,0:T(8,128)(2,1)S(1)} %get-tuple-element.9.refs_1_, f32[1,256,384]{2,1,0:T(8,128)S(1)} %get-tuple-element.10.refs_2_, ...), custom_call_target="tpu_custom_call" | custom-call | tf_op jit(solution)/shard_map/pallas_call | solution.py:534

commit v5 on v3

--- a/solution.py
+++ b/solution.py
@@ -362,6 +362,15 @@
             send(buf.at[0], buf.at[4 - i], s, r + 3 - i, dp=peer(i)).start()
         send(buf.at[0], buf.at[4], s, r_twin, dp=twin).start()
 
+    def tell_all(buf, s, r, r_twin):
+        for f in (2, 6, 1, 3, 5, 7, 4):
+            b = back(f)
+            send(buf.at[0], buf.at[b], s, r + b - 1 if f < 4 else r_twin, dp=peer(f)).start()
+
+    def heard(buf, r):
+        for i in (1, 2, 3):
+            arrived(buf.at[i], r + i - 1)
+
     def retell(buf, s, r, r_twin):
         for i in (1, 2, 3):
             arrived(buf.at[i], r + i - 1)
@@ -387,7 +396,7 @@
 
     arrived(other_dh, SWAP_DH)
     choose(other_dh, own_dh, dh_all)
-    tell(dh_all, S_DH, DH_IN, DH_TWIN)
+    tell_all(dh_all, S_DH, DH_IN, DH_TWIN)
     send_back(dx_out, dx_in, S_DX, DX)
     retell(act_all, S_ACT, ACT_IN, ACT_TWIN)
 
@@ -410,7 +419,7 @@
             send(down_out.at[p], down_in.at[4 * b + lax.rem(4 - i, 4)], S_DOWN, DOWN, dp=p).start()
 
     down_in[0] = down_out[group]
-    retell(dh_all, S_DH, DH_IN, DH_TWIN)
+    heard(dh_all, DH_IN)
     arrived(dh_all.at[pl.ds(4, 4)], DH_TWIN)
     ugrad_ref[0] = dot(x_rows[...].reshape(total, part), dh_all[...].reshape(total, fw), TN)
 

time: 30 us -> 30 us (level)
  no operation moved by 1% of the time
where the time goes in v5:
time: 30 us; the launch traced here: 29.8 us
  Pallas kernels  29.2 us (97%)
  between operations  0.64 us (2%)
    pallas_call x1, Pallas kernels, by_kernel(): pl.pallas_call(kernel, out_shape=tuple((pltpu.VMEM(*a) for a in shapes)),...  28.2 us
    pallas_call x1, Pallas kernels, by_kernel(): pl.pallas_call(place, out_shape=tuple((jax.ShapeDtypeStruct(*a) for a in...  0.99 us

profile of v5, /device:TPU:0, one launch (start us, length us, event | category | flops | bytes accessed | tf_op | source)
XLA Modules:
  0.0 29.8 jit_solution(17699874949320728834)
XLA Ops:
  0.6 28.2 %shard_map.102 = (bf16[16,2048]{1,0:T(8,128)(2,1)S(1)}, bf16[16,2048]{1,0:T(8,128)(2,1)S(1)}, f32[1,256,384]{2,1,0:T(8,128)S(1)}, f32[1,48,2048]{2,1,0:T(8,128)S(1)}) custom-call(s32[4]{0:T(128)} %swapped_hbm.1, bf16[16,2048]{1,0:T(8,128)(2,1)} %tok_ref.1, bf16[16,2048]{1,0:T(8,128)(2,1)} %og_ref.1, bf16[2,16]{1,0:T(2,128)(2,1)} %bitcast.3, ...), custom_call_target="tpu_custom_call" | custom-call | tf_op jit(solution)/shard_map/pallas_call | solution.py:498
  28.8 1.0 %shard_map.103 = (bf16[16,2048]{1,0:T(8,128)(2,1)}, bf16[16,2048]{1,0:T(8,128)(2,1)}, f32[1,256,384]{2,1,0:T(8,128)}, f32[1,48,2048]{2,1,0:T(8,128)}) custom-call(bf16[16,2048]{1,0:T(8,128)(2,1)S(1)} %get-tuple-element.8.refs_0_, bf16[16,2048]{1,0:T(8,128)(2,1)S(1)} %get-tuple-element.9.refs_1_, f32[1,256,384]{2,1,0:T(8,128)S(1)} %get-tuple-element.10.refs_2_, ...), custom_call_target="tpu_custom_call" | custom-call | tf_op jit(solution)/shard_map/pallas_call | solution.py:537
